TPU v7x, 32 devices: a whole 2x2x4 slice. The times are simulated.
32 devices in a mesh: seq: 8 (over z, y), head: 4 (over x, core).
Axes of the slice: x: 2, y: 2, z: 4, core: 2. Of those that a mesh axis runs over, the one named last changes fastest.
Arguments:
- tokens: bfloat16 [2048, 2048], P('seq')
- w_qkv: bfloat16 [2048, 3, 2048], P(None, None, 'head'), may hold values from -0.125 to 0.125
- w_out: bfloat16 [2048, 2048], P('head'), may hold values from -0.125 to 0.125
- norm_gain: float32 [2048], replicated, may hold values from 0.25 to 1.75
- w_label: bfloat16 [2048, 128], replicated, may hold values from -0.125 to 0.125
- offset_mid: int32 [16], P('head'), may hold values from 0 to 7
- offset_far: int32 [16], P('head'), may hold values from 0 to 7
Outputs:
- logits: float32 [2048, 128], P('seq')
All inputs are finite; a program needn't handle non-finite values.
Results may differ from a plain program's by a relative error of at most 0.023.
The roundings to bfloat16 on the way count: a program that leaves them out, or rounds other values in their place, can miss the bound.
Values may be sent and summed in bfloat16 or wider, within the bound.
A program may use at most 64 MiB of HBM per device.

v0:
```python
import jax
import jax.numpy as jnp
from jax import lax
from jax.sharding import PartitionSpec as P

SPAN = 8


def from_behind(block, axis, distance):
    devices = range(lax.axis_size(axis))
    route = [((i - distance) % len(devices), i) for i in devices]
    return lax.ppermute(block, axis, route)


def attend(queries, keys, values):
    scores = jnp.einsum(
        "rhe,she->hrs", queries, keys, preferred_element_type=jnp.float32
    ) / jnp.sqrt(jnp.float32(queries.shape[2]))
    top = jnp.max(scores, axis=-1)
    weights = jnp.exp(scores - top[..., None])
    total = jnp.sum(weights, axis=-1)
    summed = jnp.einsum(
        "hrs,she->rhe", weights.astype(jnp.bfloat16), values, preferred_element_type=jnp.float32
    )
    return (top.T, total.T, summed)


def select_rows(array, offsets, rate):
    rows = array.shape[0] // rate
    shaped = array.reshape(rows, rate, array.shape[1], array.shape[2])
    index = jnp.broadcast_to(
        offsets[None, None, :, None], (rows, 1, array.shape[1], array.shape[2])
    )
    return jnp.take_along_axis(shaped, index, axis=1)[:, 0]


def spread_rows(parts, offsets, rate):
    top, total, summed = parts
    rows = top.shape[0]
    marks = jnp.arange(rate, dtype=jnp.int32)[None, :, None] == offsets[None, None, :]
    top_full = jnp.where(marks, top[:, None, :], jnp.float32(-1e30)).reshape(rows * rate, -1)
    total_full = jnp.where(marks, total[:, None, :], jnp.float32(0.0)).reshape(rows * rate, -1)
    sum_full = jnp.where(marks[..., None], summed[:, None], jnp.float32(0.0)).reshape(
        rows * rate, summed.shape[1], summed.shape[2]
    )
    return (top_full, total_full, sum_full)


def body(tokens, w_qkv, w_out, norm_gain, w_label, offset_mid, offset_far):
    tok_rows = tokens.shape[0]
    local_heads = offset_mid.shape[0]
    head_size = w_qkv.shape[2] // local_heads
    qkv = jnp.einsum("td,dce->tce", tokens, w_qkv, preferred_element_type=jnp.float32).astype(
        jnp.bfloat16
    )
    qkv = qkv.reshape(tok_rows, 3, local_heads, head_size)
    queries, keys, values = (qkv[:, 0], qkv[:, 1], qkv[:, 2])
    seq_count = lax.axis_size("seq")
    near = attend(queries, keys, values)
    mid_q = select_rows(queries, offset_mid, SPAN)
    mid_kv = jnp.stack(
        [select_rows(keys, offset_mid, SPAN), select_rows(values, offset_mid, SPAN)], axis=0
    )
    mid_rows = mid_kv.shape[1]
    position = (lax.axis_index("seq") + SPAN // 2) % SPAN
    lower_pieces = []
    upper_pieces = []
    for step_back in range(1, SPAN):
        lower_pieces.insert(0, from_behind(mid_kv, "seq", step_back))
        upper_pieces.append(from_behind(mid_kv, "seq", -step_back))
    window = jnp.concatenate(lower_pieces + [mid_kv] + upper_pieces, axis=1)
    gathered = lax.dynamic_slice_in_dim(
        window, (SPAN - 1 - position) * mid_rows, SPAN * mid_rows, 1
    )
    middle = spread_rows(attend(mid_q, gathered[0], gathered[1]), offset_mid, SPAN)
    far_q = select_rows(queries, offset_far, seq_count)
    far_kv = jnp.stack(
        [select_rows(keys, offset_far, seq_count), select_rows(values, offset_far, seq_count)],
        axis=0,
    )
    far_all = lax.all_gather(far_kv, "seq", axis=1, tiled=True)
    distant = spread_rows(attend(far_q, far_all[0], far_all[1]), offset_far, seq_count)
    branches = [near, middle, distant]
    peak = jnp.maximum(jnp.maximum(near[0], middle[0]), distant[0])
    upper = jnp.zeros((tok_rows, local_heads, head_size), jnp.float32)
    lower = jnp.zeros((tok_rows, local_heads), jnp.float32)
    for top, total, summed in branches:
        factor = jnp.exp(top - peak)
        upper = upper + factor[..., None] * summed
        lower = lower + factor * total
    attn = (
        (upper / lower[..., None]).astype(jnp.bfloat16).reshape(tok_rows, local_heads * head_size)
    )
    partial_out = jnp.dot(attn, w_out, preferred_element_type=jnp.float32)
    projected = lax.psum(partial_out.astype(jnp.bfloat16), "head").astype(jnp.float32)
    mixed = tokens.astype(jnp.float32) + projected
    mean_sq = jnp.mean(mixed * mixed, axis=-1)
    scaled = (mixed * norm_gain).astype(jnp.bfloat16)
    product = jnp.dot(scaled, w_label, preferred_element_type=jnp.float32)
    return product / jnp.sqrt(mean_sq + 1e-05)[:, None]


def solution(mesh):
    return jax.shard_map(
        body,
        mesh=mesh,
        in_specs=(
            P("seq", None),
            P(None, None, "head"),
            P("head", None),
            P(),
            P(),
            P("head"),
            P("head"),
        ),
        out_specs=P("seq", None),
        check_vma=False,
    )
```

profile of v0, /device:TPU:0, one launch (start us, length us, event | category | flops | bytes accessed | tf_op | source)
XLA Modules:
  0.0 1268.6 jit_solution(2293845081796703411)
XLA Ops:
  10.4 5.8 convolution_convert_fusion.1
  16.2 1.7 reshape.147
  19.0 163.7 %gather_fusion.1 = bf16[16384]{0:T(1024)(128)(2,1)S(1)} fusion(bf16[32,8,4,128]{3,1,0,2:T(8,128)(2,1)S(1)} %get-tuple-element.26, s32[16384]{0:T(1024)S(1)} %bitcast.152), kind=kCustom, calls=%fused_computation.1.clone | custom fusion | bytes 327680 | tf_op jit(solution)/shard_map/jit(take_along_axis)/gather | solution.py:34
  182.7 163.7 %gather_fusion.2 = bf16[16384]{0:T(1024)(128)(2,1)S(1)} fusion(bf16[32,8,4,128]{3,1,0,2:T(8,128)(2,1)S(1)} %get-tuple-element.25, s32[16384]{0:T(1024)S(1)} %bitcast.153), kind=kCustom, calls=%fused_computation.2.clone | custom fusion | bytes 327680 | tf_op jit(solution)/shard_map/jit(take_along_axis)/gather | solution.py:34
  347.2 6.0 collective-permute-start
  353.7 3.0 collective-permute-start.3
  356.7 163.7 %gather_fusion.5 = bf16[16384]{0:T(1024)(128)(2,1)S(1)} fusion(bf16[32,8,4,128]{3,1,0,2:T(8,128)(2,1)S(1)} %get-tuple-element.25, s32[16384]{0:T(1024)S(1)} %bitcast.155), kind=kCustom, calls=%fused_computation.5.clone | custom fusion | bytes 327680 | tf_op jit(solution)/shard_map/jit(take_along_axis)/gather | solution.py:34
  520.5 163.7 %gather_fusion.4 = bf16[16384]{0:T(1024)(128)(2,1)S(1)} fusion(bf16[32,8,4,128]{3,1,0,2:T(8,128)(2,1)S(1)} %get-tuple-element.26, s32[16384]{0:T(1024)S(1)} %bitcast.156), kind=kCustom, calls=%fused_computation.4.clone | custom fusion | bytes 327680 | tf_op jit(solution)/shard_map/jit(take_along_axis)/gather | solution.py:34
  684.2 235.9 %gather_fusion = bf16[16384]{0:T(1024)(128)(2,1)} fusion(bf16[32,8,4,128]{3,1,0,2:T(8,128)(2,1)S(1)} %bitcast.150, s32[16384]{0:T(1024)S(1)} %bitcast.154), kind=kCustom, calls=%fused_computation.clone | custom fusion | bytes 327680 | tf_op jit(solution)/shard_map/jit(take_along_axis)/gather | solution.py:34
  920.2 236.0 %gather_fusion.3 = bf16[16384]{0:T(1024)(128)(2,1)} fusion(bf16[32,8,4,128]{3,1,0,2:T(8,128)(2,1)S(1)} %bitcast.151, s32[16384]{0:T(1024)S(1)} %bitcast.157), kind=kCustom, calls=%fused_computation.3.clone | custom fusion | bytes 327680 | tf_op jit(solution)/shard_map/jit(take_along_axis)/gather | solution.py:34
  1156.1 1.3 fusion.65
  1158.1 1.2 iota_compare_fusion
  1159.3 0.9 copy.57
  1161.0 33.1 %all_gather.3 = bf16[2,256,4,128]{3,1,2,0:T(8,128)(2,1)S(1)} all-gather(bf16[2,32,4,128]{3,1,2,0:T(8,128)(2,1)S(1)} %pad_maximum_fusion.1), channel_id=1, replica_groups=mesh['seq'=8,'head'=4] {'seq'}, dimensions={1}, use_global_device_ids=true | all-gather | bytes 589824 | tf_op jit(solution)/shard_map/all_gather | solution.py:81
  1194.0 1.1 fusion.63
  1195.4 0.9 broadcast_bitcast_fusion
  1198.4 2.0 copy.53
  1201.4 0.9 constant_dynamic-update-slice_fusion.13
  1202.2 0.9 constant_dynamic-update-slice_fusion.12
  1203.1 0.9 constant_dynamic-update-slice_fusion.11
  1204.0 0.9 constant_dynamic-update-slice_fusion.10
  1204.8 1.9 collective-permute-done.5
  1206.7 1.8 collective-permute-done.6
  1208.6 0.9 constant_dynamic-update-slice_fusion.6
  1212.9 1.0 copy-done.6
  1214.7 1.2 convolution_bitcast_fusion.2
  1216.7 2.1 copy.52
  1218.8 1.6 fusion.4
  1220.5 1.8 convolution_convert_fusion
  1222.3 34.9 %all-reduce.2.cloned.1.call-done = bf16[256,2048]{1,0:T(8,128)(2,1)} async-done(((bf16[256,2048]{1,0:T(8,128)(2,1)}), bf16[256,2048]{1,0:T(8,128)(2,1)}) %all-reduce.2.cloned.1.call-update) | async-done | bytes 1048592 | tf_op jit(solution)/shard_map/psum | solution.py:95
  1257.2 2.0 multiply_reduce_fusion
  1259.3 2.5 convolution_divide_fusion
  (86 shorter events, 16.1 us)
Async XLA Ops:
  6.5 1214.0 %copy-start = (bf16[512,2048]{1,0:T(8,128)(2,1)S(1)}, bf16[512,2048]{1,0:T(8,128)(2,1)}, u32[]{:S(2)}) copy-start(bf16[512,2048]{1,0:T(8,128)(2,1)} %param.11) | copy-start | bytes 6291460
  6.5 1250.7 %all-reduce.2.cloned.1.call-start = ((), (), s32[]{:S(2)}) async-start(), calls=%async_computation | async-start | bytes 2097152 | tf_op jit(solution)/shard_map/psum | solution.py:95
  7.3 2.9 copy-start.10
  8.0 2.2 copy-start.9
  18.2 0.7 copy-start.1
  18.2 0.8 copy-start.4
  18.3 665.9 %copy-start.3 = (bf16[256,1,4,128]{3,2,0,1:T(4,128)(2,1)}, bf16[256,1,4,128]{3,2,0,1:T(4,128)(2,1)S(1)}, u32[]{:S(2)}) copy-start(bf16[256,1,4,128]{3,2,0,1:T(4,128)(2,1)S(1)} %get-tuple-element.11) | copy-start | bytes 786436
  182.7 163.7 %copy-start.8 = (s32[4]{0:T(128)S(1)}, s32[4]{0:T(128)}, u32[]{:S(2)}) copy-start(s32[4]{0:T(128)} %param.14) | copy-start | bytes 52
  347.2 853.2 %collective-permute-start = (bf16[2,32,4,128]{3,1,2,0:T(8,128)(2,1)}, bf16[2,32,4,128]{3,1,2,0:T(8,128)(2,1)}, u32[]{:S(2)}, u32[]{:S(2)}) collective-permute-start(bf16[2,32,4,128]{3,1,2,0:T(8,128)(2,1)} %pad_maximum_fusion), channel_id=1, source_target_pairs={{4,0},{8,4},{12,8},{16,12},{20,16},{24,20},{28,24},{0,28},{5,1},{9... | collective-permute-start | bytes 196616 | tf_op jit(solution)/shard_map/ppermute | solution.py:12
  353.2 848.1 %collective-permute-start.1 = (bf16[2,32,4,128]{3,1,2,0:T(8,128)(2,1)}, bf16[2,32,4,128]{3,1,2,0:T(8,128)(2,1)}, u32[]{:S(2)}, u32[]{:S(2)}) collective-permute-start(bf16[2,32,4,128]{3,1,2,0:T(8,128)(2,1)} %pad_maximum_fusion), channel_id=1, source_target_pairs={{8,0},{12,4},{16,8},{20,12},{24,16},{28,20},{0,24},{4,28},{9,1},{1... | collective-permute-start | bytes 196616 | tf_op jit(solution)/shard_map/ppermute | solution.py:12
  353.7 848.6 %collective-permute-start.2 = (bf16[2,32,4,128]{3,1,2,0:T(8,128)(2,1)}, bf16[2,32,4,128]{3,1,2,0:T(8,128)(2,1)}, u32[]{:S(2)}, u32[]{:S(2)}) collective-permute-start(bf16[2,32,4,128]{3,1,2,0:T(8,128)(2,1)} %pad_maximum_fusion), channel_id=1, source_target_pairs={{12,0},{16,4},{20,8},{24,12},{28,16},{0,20},{4,24},{8,28},{13,1},{... | collective-permute-start | bytes 196616 | tf_op jit(solution)/shard_map/ppermute | solution.py:12
  353.7 849.4 %collective-permute-start.3 = (bf16[2,32,4,128]{3,1,2,0:T(8,128)(2,1)}, bf16[2,32,4,128]{3,1,2,0:T(8,128)(2,1)}, u32[]{:S(2)}, u32[]{:S(2)}) collective-permute-start(bf16[2,32,4,128]{3,1,2,0:T(8,128)(2,1)} %pad_maximum_fusion), channel_id=1, source_target_pairs={{16,0},{20,4},{24,8},{28,12},{0,16},{4,20},{8,24},{12,28},{17,1},{... | collective-permute-start | bytes 196616 | tf_op jit(solution)/shard_map/ppermute | solution.py:12
  356.6 847.3 %collective-permute-start.4 = (bf16[2,32,4,128]{3,1,2,0:T(8,128)(2,1)}, bf16[2,32,4,128]{3,1,2,0:T(8,128)(2,1)}, u32[]{:S(2)}, u32[]{:S(2)}) collective-permute-start(bf16[2,32,4,128]{3,1,2,0:T(8,128)(2,1)} %pad_maximum_fusion), channel_id=1, source_target_pairs={{20,0},{24,4},{28,8},{0,12},{4,16},{8,20},{12,24},{16,28},{21,1},{... | collective-permute-start | bytes 196616 | tf_op jit(solution)/shard_map/ppermute | solution.py:12
  920.2 239.1 %copy-start.2 = (bf16[256,1,4,128]{3,2,0,1:T(4,128)(2,1)S(1)}, bf16[256,1,4,128]{3,2,0,1:T(4,128)(2,1)}, u32[]{:S(2)}) copy-start(bf16[256,1,4,128]{3,2,0,1:T(4,128)(2,1)} %copy-done.1) | copy-start | bytes 786436
  1160.2 53.6 %copy-start.7 = (bf16[16384]{0:T(1024)(128)(2,1)S(1)}, bf16[16384]{0:T(1024)(128)(2,1)}, u32[]{:S(2)}) copy-start(bf16[16384]{0:T(1024)(128)(2,1)} %gather_fusion) | copy-start | bytes 98308
  1200.4 6.3 collective-permute-start.5
  1201.3 7.2 collective-permute-start.6
  1212.9 1.0 copy-start.6
  1214.6 44.6 %copy-start.11 = (f32[2048]{0:T(1024)S(1)}, f32[2048]{0:T(1024)}, u32[]{:S(2)}) copy-start(f32[2048]{0:T(1024)} %param.12) | copy-start | bytes 24580
  1220.5 38.8 %copy-start.5 = (bf16[256,2048]{1,0:T(8,128)(2,1)S(1)}, bf16[256,2048]{1,0:T(8,128)(2,1)}, u32[]{:S(2)}) copy-start(bf16[256,2048]{1,0:T(8,128)(2,1)} %param.9) | copy-start | bytes 3145732
Sparse Core Ops, SparseCore 0:
  1222.4 34.7 all-reduce.1
where the time goes:
time: 1270 us
  local copies, waits for them, and re-layouts  1150 us (91%)
  waiting for transfers between devices  38.7 us (3%)
  blocking collectives  33.1 us (3%)
  matrix products  15.8 us (1%)
  between operations  13.8 us (1%)
    gather x8, local copies, waits for them, and re-layouts, select_rows(): return jnp.take_along_axis(shaped, index, axis=1)[:, 0]  1130 us
    psum x1, waiting for transfers between devices, body(): lax.psum(partial_out.astype(jnp.bfloat16), 'head').astype(jnp.float32)  34.9 us
    all_gather x1, blocking collectives, body(): far_all = lax.all_gather(far_kv, 'seq', axis=1, tiled=True)  33.1 us
  transfers between devices with their start and end apart: 8, of which 3 were waited for; matrix products, arithmetic and copies ran while one was open for 64% of the time, Pallas kernels for 0%

commit v1 on v0

--- a/solution.py
+++ b/solution.py
@@ -1,7 +1,13 @@
+import functools
+
 import jax
 import jax.numpy as jnp
 from jax import lax
+from jax.experimental import pallas as pl
+from jax.experimental.pallas import tpu as pltpu
 from jax.sharding import PartitionSpec as P
+
+MESH = pl.DeviceIdType.MESH
 
 SPAN = 8
 
@@ -28,10 +34,8 @@
 def select_rows(array, offsets, rate):
     rows = array.shape[0] // rate
     shaped = array.reshape(rows, rate, array.shape[1], array.shape[2])
-    index = jnp.broadcast_to(
-        offsets[None, None, :, None], (rows, 1, array.shape[1], array.shape[2])
-    )
-    return jnp.take_along_axis(shaped, index, axis=1)[:, 0]
+    marks = jnp.arange(rate, dtype=jnp.int32)[None, :, None] == offsets[None, None, :]
+    return jnp.sum(jnp.where(marks[..., None], shaped, jnp.zeros_like(shaped)), axis=1)
 
 
 def spread_rows(parts, offsets, rate):
@@ -100,9 +104,356 @@
     return product / jnp.sqrt(mean_sq + 1e-05)[:, None]
 
 
+def softmax_parts(queries, keys, values):
+    scale = 1.0 / queries.shape[1] ** 0.5
+    scores = (
+        lax.dot_general(
+            queries, keys, (((1,), (1,)), ((), ())), preferred_element_type=jnp.float32
+        )
+        * scale
+    )
+    top = jnp.max(scores, axis=-1, keepdims=True)
+    weights = jnp.exp(scores - top)
+    total = jnp.sum(weights, axis=-1, keepdims=True)
+    summed = jnp.dot(weights.astype(jnp.bfloat16), values, preferred_element_type=jnp.float32)
+    return summed / total, top + jnp.log(total)
+
+
+def kernel(
+    tok_hbm, wqkv_hbm, wout_hbm, gain_hbm, wlabel_hbm, off_mid, off_far, out_ref,
+    tok, wqkv, wout, gain, wlabel, qkv, pair_out, pair_in, ret_o, ret_l, got_o, got_l,
+    attn, parts, sib_in, x_out, x_in, log_out, log_in,
+    load_sem, w_sem, a2a_send, a2a_recv, o_send, o_recv, l_send, l_recv,
+    sib_send, sib_recv, x_send, x_recv, log_send, log_recv,
+):
+    seq = lax.axis_index("seq")
+    head = lax.axis_index("head")
+    n_seq = pair_in.shape[0]
+    n_head = log_in.shape[0]
+    rows = tok.shape[0]
+    picked = pair_in.shape[1]
+    hd = got_o.shape[2]
+    heads = n_seq // 2
+    core = lax.rem(head, 2)
+    chip = head // 2
+    sibling = head + 1 - 2 * core
+    across = lax.rem(head + 2, n_head)
+
+    barrier = pltpu.get_barrier_semaphore()
+    for d in range(1, n_seq):
+        pl.semaphore_signal(
+            barrier, inc=1, device_id=(lax.rem(seq + d, n_seq), head), device_id_type=MESH
+        )
+    for d in range(1, n_head):
+        pl.semaphore_signal(
+            barrier, inc=1, device_id=(seq, lax.rem(head + d, n_head)), device_id_type=MESH
+        )
+
+    wide = wqkv.shape[2]
+    halves = qkv.shape[2] // wide
+    loads = [pltpu.make_async_copy(tok_hbm, tok, load_sem.at[0])]
+    w_loads = []
+    for half in range(halves):
+        for c in range(3):
+            k = half * 3 + c
+            w_loads.append(
+                pltpu.make_async_copy(
+                    wqkv_hbm.at[c, :, pl.ds(half * wide, wide)], wqkv.at[k], w_sem.at[k]
+                )
+            )
+    loads.append(pltpu.make_async_copy(wout_hbm, wout, load_sem.at[1]))
+    loads.append(pltpu.make_async_copy(gain_hbm, gain, load_sem.at[2]))
+    loads.append(pltpu.make_async_copy(wlabel_hbm, wlabel, load_sem.at[3]))
+    loads[0].start()
+    for load in w_loads:
+        load.start()
+    for load in loads[1:]:
+        load.start()
+
+    def pair_copy(j):
+        return pltpu.make_async_remote_copy(
+            src_ref=pair_out.at[j], dst_ref=pair_in.at[seq],
+            send_sem=a2a_send.at[j], recv_sem=a2a_recv.at[seq],
+            device_id=(j, head), device_id_type=MESH,
+        )
+
+    def pair_arrival(i):
+        return pltpu.make_async_remote_copy(
+            src_ref=pair_out.at[i], dst_ref=pair_in.at[i],
+            send_sem=a2a_send.at[i], recv_sem=a2a_recv.at[i],
+            device_id=(i, head), device_id_type=MESH,
+        )
+
+    sel_row = lax.broadcasted_iota(jnp.int32, (picked, rows), 0)
+    sel_tok = lax.broadcasted_iota(jnp.int32, (picked, rows), 1)
+    loads[0].wait()
+    for half in range(halves):
+        for c in range(3):
+            k = half * 3 + c
+            w_loads[k].wait()
+            qkv[c, :, half * wide : (half + 1) * wide] = jnp.dot(
+                tok[...], wqkv[k], preferred_element_type=jnp.float32
+            ).astype(jnp.bfloat16)
+        if half == 0:
+            pl.semaphore_wait(barrier, n_seq + n_head - 2)
+        for h in range(half * wide // hd, (half + 1) * wide // hd):
+            cols = slice(h * hd, (h + 1) * hd)
+            mine = jnp.concatenate([qkv[c, :, cols] for c in range(3)], axis=1)
+            for b, off in enumerate((off_mid, off_far)):
+                j = b * heads + h
+                one_hot = (sel_tok == sel_row * SPAN + off[h]).astype(jnp.bfloat16)
+                pair_out[j] = jnp.dot(
+                    one_hot, mine, preferred_element_type=jnp.float32
+                ).astype(jnp.bfloat16)
+
+                @pl.when(seq != j)
+                def _(j=j):
+                    pair_copy(j).start()
+
+    pair_in[seq] = pair_out[seq]
+
+    near = []
+    for h in range(heads):
+        cols = slice(h * hd, (h + 1) * hd)
+        near.append(softmax_parts(qkv[0, :, cols], qkv[1, :, cols], qkv[2, :, cols]))
+
+    for i in range(n_seq):
+
+        @pl.when(seq != i)
+        def _(i=i):
+            pair_arrival(i).wait_recv()
+
+    everyone = n_seq * picked
+    pq, pk, pv = (
+        pair_in[:, :, c * hd : (c + 1) * hd].reshape(everyone, hd) for c in range(3)
+    )
+    o, lse = softmax_parts(pq, pk, pv)
+    ret_o[...] = o.astype(jnp.bfloat16).reshape(n_seq, picked, hd)
+    r0 = lax.broadcasted_iota(jnp.int32, (everyone, everyone), 0)
+    r1 = lax.broadcasted_iota(jnp.int32, (everyone, everyone), 1)
+    lse_row = jnp.sum(jnp.where(r0 == r1, lse, 0.0), axis=0, keepdims=True)
+    per_tile = hd // picked
+    for t in range(everyone // hd):
+        ret_l[t] = jnp.broadcast_to(lse_row[:, t * hd : (t + 1) * hd], ret_l.shape[1:])
+
+    def back_copies(i, slot):
+        return (
+            pltpu.make_async_remote_copy(
+                src_ref=ret_o.at[i], dst_ref=got_o.at[slot],
+                send_sem=o_send.at[i], recv_sem=o_recv.at[slot],
+                device_id=(i, head), device_id_type=MESH,
+            ),
+            pltpu.make_async_remote_copy(
+                src_ref=ret_l.at[i // per_tile], dst_ref=got_l.at[slot],
+                send_sem=l_send.at[i], recv_sem=l_recv.at[slot],
+                device_id=(i, head), device_id_type=MESH,
+            ),
+        )
+
+    for i in range(n_seq):
+
+        @pl.when(seq != i)
+        def _(i=i):
+            for copy in back_copies(i, seq):
+                copy.start()
+
+    got_o[seq] = ret_o[seq]
+    got_l[seq] = ret_l[seq // per_tile]
+
+    tok_col = lax.broadcasted_iota(jnp.int32, (rows, hd), 0)
+    lane = lax.broadcasted_iota(jnp.int32, (rows, hd), 1)
+    base = lax.rem(seq, per_tile) * picked
+    tok_sel = lax.broadcasted_iota(jnp.int32, (rows, picked), 0)
+    row_sel = lax.broadcasted_iota(jnp.int32, (rows, picked), 1)
+    tok_one = lax.broadcasted_iota(jnp.int32, (rows, 1), 0)
+    for h in range(heads):
+        terms = [near[h]]
+        marks = [None]
+        for b, off in enumerate((off_mid, off_far)):
+            j = b * heads + h
+
+            @pl.when(seq != j)
+            def _(j=j):
+                for copy in back_copies(j, j):
+                    copy.wait_recv()
+
+            spot = off[h]
+            hit = (lane - base) * SPAN + spot == tok_col
+            lse_col = jnp.sum(
+                jnp.where(hit, got_l[j, 0:1, :], 0.0), axis=-1, keepdims=True
+            )
+            one_hot = (tok_sel == row_sel * SPAN + spot).astype(jnp.bfloat16)
+            spread = jnp.dot(one_hot, got_o[j], preferred_element_type=jnp.float32)
+            mark = lax.rem(tok_one, SPAN) == spot
+            terms.append((spread, jnp.where(mark, lse_col, -1e30)))
+            marks.append(mark)
+        peak = jnp.maximum(jnp.maximum(terms[0][1], terms[1][1]), terms[2][1])
+        upper = jnp.zeros((rows, hd), jnp.float32)
+        lower = jnp.zeros((rows, 1), jnp.float32)
+        for (o, lse), mark in zip(terms, marks):
+            factor = jnp.exp(lse - peak)
+            if mark is not None:
+                factor = jnp.where(mark, factor, 0.0)
+            upper = upper + factor * o
+            lower = lower + factor
+        attn[:, h * hd : (h + 1) * hd] = (upper / lower).astype(jnp.bfloat16)
+
+    chunks = x_in.shape[0]
+    part = x_in.shape[1]
+    width = x_in.shape[2]
+
+    def sib_copy(s, n):
+        return pltpu.make_async_remote_copy(
+            src_ref=parts.at[s, n, 1 - core], dst_ref=sib_in.at[s, n],
+            send_sem=sib_send.at[s, n], recv_sem=sib_recv.at[s, n],
+            device_id=(seq, sibling), device_id_type=MESH,
+        )
+
+    def x_copy(n):
+        return pltpu.make_async_remote_copy(
+            src_ref=x_out.at[n], dst_ref=x_in.at[n],
+            send_sem=x_send.at[n], recv_sem=x_recv.at[n],
+            device_id=(seq, across), device_id_type=MESH,
+        )
+
+    for load in loads[1:]:
+        load.wait()
+    for s in range(2):
+        place = (1 - chip) if s == 0 else chip
+        left = attn[pl.ds(pl.multiple_of(place * 2 * part, 2 * part), 2 * part), :]
+        for n in range(chunks):
+            parts[s, n] = (
+                jnp.dot(
+                    left, wout[:, n * width : (n + 1) * width],
+                    preferred_element_type=jnp.float32,
+                )
+                .astype(jnp.bfloat16)
+                .reshape(2, part, width)
+            )
+            sib_copy(s, n).start()
+        if s == 0:
+            for n in range(chunks):
+                sib_copy(0, n).wait_recv()
+                x_out[n] = (
+                    parts[0, n, core].astype(jnp.float32) + sib_in[0, n].astype(jnp.float32)
+                ).astype(jnp.bfloat16)
+                x_copy(n).start()
+
+    squares = jnp.zeros((part, 1), jnp.float32)
+    product = jnp.zeros((part, wlabel.shape[1]), jnp.float32)
+    here = pl.ds(pl.multiple_of(head * part, part), part)
+    for n in range(chunks):
+        cols = slice(n * width, (n + 1) * width)
+        sib_copy(1, n).wait_recv()
+        x_copy(n).wait_recv()
+        summed = parts[1, n, core].astype(jnp.float32) + sib_in[1, n].astype(jnp.float32)
+        mixed = tok[here, cols].astype(jnp.float32) + (summed + x_in[n].astype(jnp.float32))
+        squares = squares + jnp.sum(mixed * mixed, axis=-1, keepdims=True)
+        scaled = (mixed * gain[:, cols]).astype(jnp.bfloat16)
+        product = product + jnp.dot(scaled, wlabel[cols, :], preferred_element_type=jnp.float32)
+    log_out[...] = product / jnp.sqrt(squares / tok.shape[1] + 1e-05)
+
+    def log_copy(p, slot):
+        return pltpu.make_async_remote_copy(
+            src_ref=log_out, dst_ref=log_in.at[slot],
+            send_sem=log_send.at[p], recv_sem=log_recv.at[slot],
+            device_id=(seq, p), device_id_type=MESH,
+        )
+
+    for p in range(n_head):
+
+        @pl.when(head != p)
+        def _(p=p):
+            log_copy(p, head).start()
+
+    log_in[head] = log_out[...]
+    for p in range(n_head):
+
+        @pl.when(head != p)
+        def _(p=p):
+            log_copy(p, p).wait_recv()
+
+        out_ref[p * part : (p + 1) * part, :] = log_in[p]
+
+    for j in range(n_seq):
+
+        @pl.when(seq != j)
+        def _(j=j):
+            pair_copy(j).wait_send()
+            for copy in back_copies(j, seq):
+                copy.wait_send()
+
+    for n in range(chunks):
+        sib_copy(0, n).wait_send()
+        sib_copy(1, n).wait_send()
+        x_copy(n).wait_send()
+    for p in range(n_head):
+
+        @pl.when(head != p)
+        def _(p=p):
+            log_copy(p, head).wait_send()
+
+
+def fused_body(n_seq, n_head, tokens, w_qkv, w_out, norm_gain, w_label, offset_mid, offset_far):
+    rows, width = tokens.shape
+    heads = offset_mid.shape[0]
+    own = w_qkv.shape[2]
+    hd = own // heads
+    classes = w_label.shape[1]
+    picked = rows // SPAN
+    part = rows // n_head
+    chunks = 4
+    span = width // chunks
+    bf16, f32 = jnp.bfloat16, jnp.float32
+    dma = pltpu.SemaphoreType.DMA
+    anywhere = pl.BlockSpec(memory_space=pl.ANY)
+    scalars = pl.BlockSpec(memory_space=pltpu.SMEM)
+    return pl.pallas_call(
+        kernel,
+        out_shape=jax.ShapeDtypeStruct((rows, classes), f32),
+        in_specs=[anywhere] * 5 + [scalars] * 2,
+        out_specs=pl.BlockSpec(memory_space=pltpu.VMEM),
+        scratch_shapes=[
+            pltpu.VMEM((rows, width), bf16),
+            pltpu.VMEM((6, width, own // 2), bf16),
+            pltpu.VMEM((own, width), bf16),
+            pltpu.VMEM((1, width), f32),
+            pltpu.VMEM((width, classes), bf16),
+            pltpu.VMEM((3, rows, own), bf16),
+            pltpu.VMEM((n_seq, picked, 3 * hd), bf16),
+            pltpu.VMEM((n_seq, picked, 3 * hd), bf16),
+            pltpu.VMEM((n_seq, picked, hd), bf16),
+            pltpu.VMEM((n_seq * picked // hd, 8, hd), f32),
+            pltpu.VMEM((n_seq, picked, hd), bf16),
+            pltpu.VMEM((n_seq, 8, hd), f32),
+            pltpu.VMEM((rows, own), bf16),
+            pltpu.VMEM((2, chunks, 2, part, span), bf16),
+            pltpu.VMEM((2, chunks, part, span), bf16),
+            pltpu.VMEM((chunks, part, span), bf16),
+            pltpu.VMEM((chunks, part, span), bf16),
+            pltpu.VMEM((part, classes), f32),
+            pltpu.VMEM((n_head, part, classes), f32),
+            dma((4,)), dma((6,)), dma((n_seq,)), dma((n_seq,)),
+            dma((n_seq,)), dma((n_seq,)), dma((n_seq,)), dma((n_seq,)),
+            dma((2, chunks)), dma((2, chunks)), dma((chunks,)), dma((chunks,)),
+            dma((n_head,)), dma((n_head,)),
+        ],
+        compiler_params=pltpu.CompilerParams(
+            collective_id=0, has_side_effects=True, vmem_limit_bytes=56 * 2**20
+        ),
+    )(
+        tokens, jnp.transpose(w_qkv, (1, 0, 2)), w_out, norm_gain[None, :], w_label,
+        offset_mid, offset_far,
+    )
+
+
 def solution(mesh):
+    n_seq, n_head = mesh.shape["seq"], mesh.shape["head"]
+    run = body
+    if n_seq == SPAN and n_head == 4:
+        run = functools.partial(fused_body, n_seq, n_head)
     return jax.shard_map(
-        body,
+        run,
         mesh=mesh,
         in_specs=(
             P("seq", None),

time: 1270 us -> 35.6 us (0.03)
  local copies, waits for them, and re-layouts: 1150 us -> 1.57 us
  waiting for transfers between devices: 38.7 us -> 0 us
  Pallas kernels: 0 us -> 33.8 us
  blocking collectives: 33.1 us -> 0 us
  matrix products: 15.8 us -> 0 us
  between operations: 13.8 us -> 0.01 us
    gather x8 -> x0, local copies, waits for them, and re-layouts: 1130 us -> none  [select_rows(): return jnp.take_along_axis(shaped, index, axis=1)[:, 0]]
    psum x1 -> x0, waiting for transfers between devices: 34.9 us -> none  [body(): lax.psum(partial_out.astype(jnp.bfloat16), 'head').astype(jnp.float32)]
    pallas_call x0 -> x1, Pallas kernels: none -> 33.8 us  [fused_body(): pl.pallas_call(kernel, out_shape=jax.ShapeDtypeStruct((rows, classes), f3...]
    all_gather x1 -> x0, blocking collectives: 33.1 us -> none  [body(): far_all = lax.all_gather(far_kv, 'seq', axis=1, tiled=True)]
    dot_general x9 -> x0, matrix products: 15.8 us -> none  [the longest x1 5.81 us: body(): jnp.einsum('td,dce->tce', tokens, w_qkv, preferred_element_type=jnp.float32)]
  transfers between devices with their start and end apart: 8 -> 0, of which waited for: 3 -> 0; matrix products, arithmetic and copies ran while one was open for 64% -> 0% of each run, Pallas kernels for 0% -> 0%
where the time goes in v1:
time: 35.6 us; the launch traced here: 35.4 us
  Pallas kernels  33.8 us (95%)
  local copies, waits for them, and re-layouts  1.57 us (4%)
    pallas_call x1, Pallas kernels, fused_body(): pl.pallas_call(kernel, out_shape=jax.ShapeDtypeStruct((rows, classes), f3...  33.8 us
    unnamed x1, local copies, waits for them, and re-layouts  1.57 us

profile of v1, /device:TPU:0, one launch (start us, length us, event | category | flops | bytes accessed | tf_op | source)
XLA Modules:
  0.0 35.4 jit_solution(14056570301155819682)
XLA Ops:
  0.0 33.8 %shard_map.73 = f32[256,128]{1,0:T(8,128)} custom-call(bf16[256,2048]{1,0:T(8,128)(2,1)} %tok_hbm.1, bf16[3,2048,512]{2,1,0:T(8,128)(2,1)} %bitcast.2, bf16[512,2048]{1,0:T(8,128)(2,1)} %wout_hbm.1, f32[1,2048]{1,0:T(1,128)} %bitcast.3, bf16[2048,128]{1,0:T(8,128)(2,1)} %wlabel_hbm.1, s32[4]{0:T(128)} %off_mid.1, s32[4]{0:T(128)} %off_far.1), custom_call_target="tpu_custom_call" | custom-call | tf_op jit(solution)/shard_map/pallas_call | solution.py:411
  33.9 1.6 %copy.9 = f32[256,128]{1,0:T(8,128)} copy(f32[256,128]{1,0:T(8,128)} %shard_map.73) | data formatting | bytes 262144

commit v2 on v1

--- a/solution.py
+++ b/solution.py
@@ -167,8 +167,6 @@
     loads[0].start()
     for load in w_loads:
         load.start()
-    for load in loads[1:]:
-        load.start()
 
     def pair_copy(j):
         return pltpu.make_async_remote_copy(
@@ -184,8 +182,10 @@
             device_id=(i, head), device_id_type=MESH,
         )
 
-    sel_row = lax.broadcasted_iota(jnp.int32, (picked, rows), 0)
-    sel_tok = lax.broadcasted_iota(jnp.int32, (picked, rows), 1)
+    both = lax.broadcasted_iota(jnp.int32, (2 * picked, rows), 0)
+    is_mid = both < picked
+    sel_row = jnp.where(is_mid, both, both - picked) * SPAN
+    sel_tok = lax.broadcasted_iota(jnp.int32, (2 * picked, rows), 1)
     loads[0].wait()
     for half in range(halves):
         for c in range(3):
@@ -194,17 +194,22 @@
             qkv[c, :, half * wide : (half + 1) * wide] = jnp.dot(
                 tok[...], wqkv[k], preferred_element_type=jnp.float32
             ).astype(jnp.bfloat16)
+        if half == halves - 1:
+            for load in loads[1:]:
+                load.start()
         if half == 0:
             pl.semaphore_wait(barrier, n_seq + n_head - 2)
         for h in range(half * wide // hd, (half + 1) * wide // hd):
             cols = slice(h * hd, (h + 1) * hd)
             mine = jnp.concatenate([qkv[c, :, cols] for c in range(3)], axis=1)
-            for b, off in enumerate((off_mid, off_far)):
+            spot = sel_row + jnp.where(is_mid, off_mid[h], off_far[h])
+            one_hot = (sel_tok == spot).astype(jnp.bfloat16)
+            found = jnp.dot(one_hot, mine, preferred_element_type=jnp.float32).astype(
+                jnp.bfloat16
+            )
+            for b in range(2):
                 j = b * heads + h
-                one_hot = (sel_tok == sel_row * SPAN + off[h]).astype(jnp.bfloat16)
-                pair_out[j] = jnp.dot(
-                    one_hot, mine, preferred_element_type=jnp.float32
-                ).astype(jnp.bfloat16)
+                pair_out[j] = found[b * picked : (b + 1) * picked]
 
                 @pl.when(seq != j)
                 def _(j=j):
@@ -212,10 +217,17 @@
 
     pair_in[seq] = pair_out[seq]
 
+    chunks = x_in.shape[0]
+    part = x_in.shape[1]
+    width = x_in.shape[2]
+    side = 2 * part
     near = []
-    for h in range(heads):
-        cols = slice(h * hd, (h + 1) * hd)
-        near.append(softmax_parts(qkv[0, :, cols], qkv[1, :, cols], qkv[2, :, cols]))
+    for s in range(2):
+        first = ((1 - chip) if s == 0 else chip) * side
+        place = pl.ds(pl.multiple_of(first, side), side)
+        for h in range(heads):
+            cols = slice(h * hd, (h + 1) * hd)
+            near.append(softmax_parts(qkv[0, place, cols], qkv[1, :, cols], qkv[2, :, cols]))
 
     for i in range(n_seq):
 
@@ -229,78 +241,82 @@
     )
     o, lse = softmax_parts(pq, pk, pv)
     ret_o[...] = o.astype(jnp.bfloat16).reshape(n_seq, picked, hd)
+    per_tile = hd // picked
+
+    def o_copy(i, slot):
+        return pltpu.make_async_remote_copy(
+            src_ref=ret_o.at[i], dst_ref=got_o.at[slot],
+            send_sem=o_send.at[i], recv_sem=o_recv.at[slot],
+            device_id=(i, head), device_id_type=MESH,
+        )
+
+    def l_copy(i, slot):
+        return pltpu.make_async_remote_copy(
+            src_ref=ret_l.at[i // per_tile], dst_ref=got_l.at[slot],
+            send_sem=l_send.at[i], recv_sem=l_recv.at[slot],
+            device_id=(i, head), device_id_type=MESH,
+        )
+
+    for i in range(n_seq):
+
+        @pl.when(seq != i)
+        def _(i=i):
+            o_copy(i, seq).start()
+
     r0 = lax.broadcasted_iota(jnp.int32, (everyone, everyone), 0)
     r1 = lax.broadcasted_iota(jnp.int32, (everyone, everyone), 1)
     lse_row = jnp.sum(jnp.where(r0 == r1, lse, 0.0), axis=0, keepdims=True)
-    per_tile = hd // picked
     for t in range(everyone // hd):
-        ret_l[t] = jnp.broadcast_to(lse_row[:, t * hd : (t + 1) * hd], ret_l.shape[1:])
-
-    def back_copies(i, slot):
-        return (
-            pltpu.make_async_remote_copy(
-                src_ref=ret_o.at[i], dst_ref=got_o.at[slot],
-                send_sem=o_send.at[i], recv_sem=o_recv.at[slot],
-                device_id=(i, head), device_id_type=MESH,
-            ),
-            pltpu.make_async_remote_copy(
-                src_ref=ret_l.at[i // per_tile], dst_ref=got_l.at[slot],
-                send_sem=l_send.at[i], recv_sem=l_recv.at[slot],
-                device_id=(i, head), device_id_type=MESH,
-            ),
-        )
-
+        ret_l[t] = lse_row[:, t * hd : (t + 1) * hd]
     for i in range(n_seq):
 
         @pl.when(seq != i)
         def _(i=i):
-            for copy in back_copies(i, seq):
-                copy.start()
+            l_copy(i, seq).start()
 
     got_o[seq] = ret_o[seq]
     got_l[seq] = ret_l[seq // per_tile]
 
-    tok_col = lax.broadcasted_iota(jnp.int32, (rows, hd), 0)
-    lane = lax.broadcasted_iota(jnp.int32, (rows, hd), 1)
     base = lax.rem(seq, per_tile) * picked
-    tok_sel = lax.broadcasted_iota(jnp.int32, (rows, picked), 0)
-    row_sel = lax.broadcasted_iota(jnp.int32, (rows, picked), 1)
-    tok_one = lax.broadcasted_iota(jnp.int32, (rows, 1), 0)
-    for h in range(heads):
-        terms = [near[h]]
-        marks = [None]
-        for b, off in enumerate((off_mid, off_far)):
-            j = b * heads + h
-
-            @pl.when(seq != j)
-            def _(j=j):
-                for copy in back_copies(j, j):
-                    copy.wait_recv()
-
-            spot = off[h]
-            hit = (lane - base) * SPAN + spot == tok_col
-            lse_col = jnp.sum(
-                jnp.where(hit, got_l[j, 0:1, :], 0.0), axis=-1, keepdims=True
-            )
-            one_hot = (tok_sel == row_sel * SPAN + spot).astype(jnp.bfloat16)
-            spread = jnp.dot(one_hot, got_o[j], preferred_element_type=jnp.float32)
-            mark = lax.rem(tok_one, SPAN) == spot
-            terms.append((spread, jnp.where(mark, lse_col, -1e30)))
-            marks.append(mark)
-        peak = jnp.maximum(jnp.maximum(terms[0][1], terms[1][1]), terms[2][1])
-        upper = jnp.zeros((rows, hd), jnp.float32)
-        lower = jnp.zeros((rows, 1), jnp.float32)
-        for (o, lse), mark in zip(terms, marks):
-            factor = jnp.exp(lse - peak)
-            if mark is not None:
-                factor = jnp.where(mark, factor, 0.0)
-            upper = upper + factor * o
-            lower = lower + factor
-        attn[:, h * hd : (h + 1) * hd] = (upper / lower).astype(jnp.bfloat16)
-
-    chunks = x_in.shape[0]
-    part = x_in.shape[1]
-    width = x_in.shape[2]
+
+    def merge(s, first):
+        tok_col = lax.broadcasted_iota(jnp.int32, (side, hd), 0) + first
+        lane = lax.broadcasted_iota(jnp.int32, (side, hd), 1) - base
+        tok_sel = lax.broadcasted_iota(jnp.int32, (side, picked), 0) + first
+        row_sel = lax.broadcasted_iota(jnp.int32, (side, picked), 1)
+        tok_one = lax.broadcasted_iota(jnp.int32, (side, 1), 0)
+        merged = []
+        for h in range(heads):
+            terms = [near[s * heads + h]]
+            marks = [None]
+            for b, off in enumerate((off_mid, off_far)):
+                j = b * heads + h
+                if s == 0:
+
+                    @pl.when(seq != j)
+                    def _(j=j):
+                        o_copy(j, j).wait_recv()
+                        l_copy(j, j).wait_recv()
+
+                spot = off[h]
+                hit = lane * SPAN + spot == tok_col
+                lse_col = jnp.sum(jnp.where(hit, got_l[j], 0.0), axis=-1, keepdims=True)
+                one_hot = (tok_sel == row_sel * SPAN + spot).astype(jnp.bfloat16)
+                spread = jnp.dot(one_hot, got_o[j], preferred_element_type=jnp.float32)
+                mark = lax.rem(tok_one, SPAN) == spot
+                terms.append((spread, jnp.where(mark, lse_col, -1e30)))
+                marks.append(mark)
+            peak = jnp.maximum(jnp.maximum(terms[0][1], terms[1][1]), terms[2][1])
+            upper = jnp.zeros((side, hd), jnp.float32)
+            lower = jnp.zeros((side, 1), jnp.float32)
+            for (o, lse), mark in zip(terms, marks):
+                factor = jnp.exp(lse - peak)
+                if mark is not None:
+                    factor = jnp.where(mark, factor, 0.0)
+                upper = upper + factor * o
+                lower = lower + factor
+            merged.append((upper / lower).astype(jnp.bfloat16))
+        return jnp.concatenate(merged, axis=1)
 
     def sib_copy(s, n):
         return pltpu.make_async_remote_copy(
@@ -316,28 +332,31 @@
             device_id=(seq, across), device_id_type=MESH,
         )
 
+    def pass_on(n):
+        sib_copy(0, n).wait_recv()
+        x_out[n] = (
+            parts[0, n, core].astype(jnp.float32) + sib_in[0, n].astype(jnp.float32)
+        ).astype(jnp.bfloat16)
+        x_copy(n).start()
+
     for load in loads[1:]:
         load.wait()
     for s in range(2):
-        place = (1 - chip) if s == 0 else chip
-        left = attn[pl.ds(pl.multiple_of(place * 2 * part, 2 * part), 2 * part), :]
+        attn[s] = merge(s, ((1 - chip) if s == 0 else chip) * side)
         for n in range(chunks):
             parts[s, n] = (
                 jnp.dot(
-                    left, wout[:, n * width : (n + 1) * width],
+                    attn[s], wout[:, n * width : (n + 1) * width],
                     preferred_element_type=jnp.float32,
                 )
                 .astype(jnp.bfloat16)
                 .reshape(2, part, width)
             )
             sib_copy(s, n).start()
+            if s == 0 and n > 0:
+                pass_on(n - 1)
         if s == 0:
-            for n in range(chunks):
-                sib_copy(0, n).wait_recv()
-                x_out[n] = (
-                    parts[0, n, core].astype(jnp.float32) + sib_in[0, n].astype(jnp.float32)
-                ).astype(jnp.bfloat16)
-                x_copy(n).start()
+            pass_on(chunks - 1)
 
     squares = jnp.zeros((part, 1), jnp.float32)
     product = jnp.zeros((part, wlabel.shape[1]), jnp.float32)
@@ -351,7 +370,7 @@
         squares = squares + jnp.sum(mixed * mixed, axis=-1, keepdims=True)
         scaled = (mixed * gain[:, cols]).astype(jnp.bfloat16)
         product = product + jnp.dot(scaled, wlabel[cols, :], preferred_element_type=jnp.float32)
-    log_out[...] = product / jnp.sqrt(squares / tok.shape[1] + 1e-05)
+    log_out[...] = (product / jnp.sqrt(squares / tok.shape[1] + 1e-05)).astype(jnp.bfloat16)
 
     def log_copy(p, slot):
         return pltpu.make_async_remote_copy(
@@ -380,8 +399,8 @@
         @pl.when(seq != j)
         def _(j=j):
             pair_copy(j).wait_send()
-            for copy in back_copies(j, seq):
-                copy.wait_send()
+            o_copy(j, seq).wait_send()
+            l_copy(j, seq).wait_send()
 
     for n in range(chunks):
         sib_copy(0, n).wait_send()
@@ -410,7 +429,7 @@
     scalars = pl.BlockSpec(memory_space=pltpu.SMEM)
     return pl.pallas_call(
         kernel,
-        out_shape=jax.ShapeDtypeStruct((rows, classes), f32),
+        out_shape=pltpu.VMEM((rows, classes), bf16),
         in_specs=[anywhere] * 5 + [scalars] * 2,
         out_specs=pl.BlockSpec(memory_space=pltpu.VMEM),
         scratch_shapes=[
@@ -423,16 +442,16 @@
             pltpu.VMEM((n_seq, picked, 3 * hd), bf16),
             pltpu.VMEM((n_seq, picked, 3 * hd), bf16),
             pltpu.VMEM((n_seq, picked, hd), bf16),
-            pltpu.VMEM((n_seq * picked // hd, 8, hd), f32),
+            pltpu.VMEM((n_seq * picked // hd, 1, hd), f32),
             pltpu.VMEM((n_seq, picked, hd), bf16),
-            pltpu.VMEM((n_seq, 8, hd), f32),
-            pltpu.VMEM((rows, own), bf16),
+            pltpu.VMEM((n_seq, 1, hd), f32),
+            pltpu.VMEM((2, 2 * part, own), bf16),
             pltpu.VMEM((2, chunks, 2, part, span), bf16),
             pltpu.VMEM((2, chunks, part, span), bf16),
             pltpu.VMEM((chunks, part, span), bf16),
             pltpu.VMEM((chunks, part, span), bf16),
-            pltpu.VMEM((part, classes), f32),
-            pltpu.VMEM((n_head, part, classes), f32),
+            pltpu.VMEM((part, classes), bf16),
+            pltpu.VMEM((n_head, part, classes), bf16),
             dma((4,)), dma((6,)), dma((n_seq,)), dma((n_seq,)),
             dma((n_seq,)), dma((n_seq,)), dma((n_seq,)), dma((n_seq,)),
             dma((2, chunks)), dma((2, chunks)), dma((chunks,)), dma((chunks,)),
@@ -444,7 +463,7 @@
     )(
         tokens, jnp.transpose(w_qkv, (1, 0, 2)), w_out, norm_gain[None, :], w_label,
         offset_mid, offset_far,
-    )
+    ).astype(f32)
 
 
 def solution(mesh):

time: 35.6 us -> 33.9 us (0.952)
  local copies, waits for them, and re-layouts: 1.57 us -> 0 us
  Pallas kernels: 33.8 us -> 33.1 us
  other arithmetic: 0 us -> 0.67 us
    unnamed x1 -> x0, local copies, waits for them, and re-layouts: 1.57 us -> none
    pallas_call x1, Pallas kernels: 33.8 us -> 33.1 us  [fused_body(): pl.pallas_call(kernel, out_shape=pltpu.VMEM((rows, classes), bf16), in_sp...]
    convert_element_type x0 -> x1, other arithmetic: none -> 0.67 us  [fused_body(): return pl.pallas_call(kernel, out_shape=pltpu.VMEM((rows, classes), bf16)...]
where the time goes in v2:
time: 33.9 us; the launch traced here: 33.8 us
  Pallas kernels  33.1 us (98%)
  other arithmetic  0.67 us (2%)
    pallas_call x1, Pallas kernels, fused_body(): pl.pallas_call(kernel, out_shape=pltpu.VMEM((rows, classes), bf16), in_sp...  33.1 us

profile of v2, /device:TPU:0, one launch (start us, length us, event | category | flops | bytes accessed | tf_op | source)
XLA Modules:
  0.0 33.8 jit_solution(11914886600451414816)
XLA Ops:
  0.0 33.1 %shard_map.73 = bf16[256,128]{1,0:T(8,128)(2,1)S(1)} custom-call(bf16[256,2048]{1,0:T(8,128)(2,1)} %tok_hbm.1, bf16[3,2048,512]{2,1,0:T(8,128)(2,1)} %bitcast.2, bf16[512,2048]{1,0:T(8,128)(2,1)} %wout_hbm.1, f32[1,2048]{1,0:T(1,128)} %bitcast.3, bf16[2048,128]{1,0:T(8,128)(2,1)} %wlabel_hbm.1, s32[4]{0:T(128)} %off_mid.1, s32[4]{0:T(128)} %off_far.1), custom_call_target="tpu_custom_call" | custom-call | tf_op jit(solution)/shard_map/pallas_call | solution.py:430
  33.1 0.7 %convert_element_type.3 = f32[256,128]{1,0:T(8,128)} convert(bf16[256,128]{1,0:T(8,128)(2,1)S(1)} %shard_map.73) | non-fusion elementwise | flops 32768 | bytes 196608 | tf_op jit(solution)/shard_map/convert_element_type | solution.py:466

commit v3 on v2

--- a/solution.py
+++ b/solution.py
@@ -210,10 +210,14 @@
             for b in range(2):
                 j = b * heads + h
                 pair_out[j] = found[b * picked : (b + 1) * picked]
-
-                @pl.when(seq != j)
-                def _(j=j):
-                    pair_copy(j).start()
+        ready = heads // halves
+        for d in range(2 * ready):
+            turn = lax.rem(seq + d, 2 * ready)
+            j = turn // ready * heads + half * ready + lax.rem(turn, ready)
+
+            @pl.when(seq != j)
+            def _(j=j):
+                pair_copy(j).start()
 
     pair_in[seq] = pair_out[seq]
 
@@ -221,19 +225,17 @@
     part = x_in.shape[1]
     width = x_in.shape[2]
     side = 2 * part
-    near = []
-    for s in range(2):
-        first = ((1 - chip) if s == 0 else chip) * side
-        place = pl.ds(pl.multiple_of(first, side), side)
-        for h in range(heads):
-            cols = slice(h * hd, (h + 1) * hd)
-            near.append(softmax_parts(qkv[0, place, cols], qkv[1, :, cols], qkv[2, :, cols]))
-
-    for i in range(n_seq):
-
-        @pl.when(seq != i)
-        def _(i=i):
-            pair_arrival(i).wait_recv()
+    firsts = ((1 - chip) * side, chip * side)
+
+    def near_rows(s, h):
+        place = pl.ds(pl.multiple_of(firsts[s], side), side)
+        cols = slice(h * hd, (h + 1) * hd)
+        return softmax_parts(qkv[0, place, cols], qkv[1, :, cols], qkv[2, :, cols])
+
+    near = [[near_rows(0, h) for h in range(heads // 2)], []]
+
+    for d in range(1, n_seq):
+        pair_arrival(lax.rem(seq + d, n_seq)).wait_recv()
 
     everyone = n_seq * picked
     pq, pk, pv = (
@@ -257,25 +259,21 @@
             device_id=(i, head), device_id_type=MESH,
         )
 
-    for i in range(n_seq):
-
-        @pl.when(seq != i)
-        def _(i=i):
-            o_copy(i, seq).start()
+    outward = sorted(range(1, n_seq), key=lambda d: abs(2 * d - n_seq))
+    for d in outward:
+        o_copy(lax.rem(seq + d, n_seq), seq).start()
 
     r0 = lax.broadcasted_iota(jnp.int32, (everyone, everyone), 0)
     r1 = lax.broadcasted_iota(jnp.int32, (everyone, everyone), 1)
     lse_row = jnp.sum(jnp.where(r0 == r1, lse, 0.0), axis=0, keepdims=True)
     for t in range(everyone // hd):
         ret_l[t] = lse_row[:, t * hd : (t + 1) * hd]
-    for i in range(n_seq):
-
-        @pl.when(seq != i)
-        def _(i=i):
-            l_copy(i, seq).start()
+    for d in outward:
+        l_copy(lax.rem(seq + d, n_seq), seq).start()
 
     got_o[seq] = ret_o[seq]
     got_l[seq] = ret_l[seq // per_tile]
+    near[0] += [near_rows(0, h) for h in range(heads // 2, heads)]
 
     base = lax.rem(seq, per_tile) * picked
 
@@ -287,17 +285,10 @@
         tok_one = lax.broadcasted_iota(jnp.int32, (side, 1), 0)
         merged = []
         for h in range(heads):
-            terms = [near[s * heads + h]]
+            terms = [near[s][h]]
             marks = [None]
             for b, off in enumerate((off_mid, off_far)):
                 j = b * heads + h
-                if s == 0:
-
-                    @pl.when(seq != j)
-                    def _(j=j):
-                        o_copy(j, j).wait_recv()
-                        l_copy(j, j).wait_recv()
-
                 spot = off[h]
                 hit = lane * SPAN + spot == tok_col
                 lse_col = jnp.sum(jnp.where(hit, got_l[j], 0.0), axis=-1, keepdims=True)
@@ -341,8 +332,14 @@
 
     for load in loads[1:]:
         load.wait()
+    for d in range(1, n_seq):
+        j = lax.rem(seq + d, n_seq)
+        o_copy(j, j).wait_recv()
+        l_copy(j, j).wait_recv()
     for s in range(2):
-        attn[s] = merge(s, ((1 - chip) if s == 0 else chip) * side)
+        if s == 1:
+            near[1] = [near_rows(1, h) for h in range(heads)]
+        attn[s] = merge(s, firsts[s])
         for n in range(chunks):
             parts[s, n] = (
                 jnp.dot(
@@ -379,38 +376,27 @@
             device_id=(seq, p), device_id_type=MESH,
         )
 
+    for d in (2, 1, 3):
+        log_copy(lax.rem(head + d, n_head), head).start()
+    log_in[head] = log_out[...]
+    for d in range(1, n_head):
+        p = lax.rem(head + d, n_head)
+        log_copy(p, p).wait_recv()
     for p in range(n_head):
-
-        @pl.when(head != p)
-        def _(p=p):
-            log_copy(p, head).start()
-
-    log_in[head] = log_out[...]
-    for p in range(n_head):
-
-        @pl.when(head != p)
-        def _(p=p):
-            log_copy(p, p).wait_recv()
-
         out_ref[p * part : (p + 1) * part, :] = log_in[p]
 
-    for j in range(n_seq):
-
-        @pl.when(seq != j)
-        def _(j=j):
-            pair_copy(j).wait_send()
-            o_copy(j, seq).wait_send()
-            l_copy(j, seq).wait_send()
+    for d in range(1, n_seq):
+        j = lax.rem(seq + d, n_seq)
+        pair_copy(j).wait_send()
+        o_copy(j, seq).wait_send()
+        l_copy(j, seq).wait_send()
 
     for n in range(chunks):
         sib_copy(0, n).wait_send()
         sib_copy(1, n).wait_send()
         x_copy(n).wait_send()
-    for p in range(n_head):
-
-        @pl.when(head != p)
-        def _(p=p):
-            log_copy(p, head).wait_send()
+    for d in range(1, n_head):
+        log_copy(lax.rem(head + d, n_head), head).wait_send()
 
 
 def fused_body(n_seq, n_head, tokens, w_qkv, w_out, norm_gain, w_label, offset_mid, offset_far):

time: 33.9 us -> 34.2 us (level)
  no operation moved by 1% of the time
where the time goes in v3:
time: 34.2 us; the launch traced here: 34.1 us
  Pallas kernels  33.4 us (98%)
  other arithmetic  0.67 us (2%)
    pallas_call x1, Pallas kernels, fused_body(): pl.pallas_call(kernel, out_shape=pltpu.VMEM((rows, classes), bf16), in_sp...  33.4 us

profile of v3, /device:TPU:0, one launch (start us, length us, event | category | flops | bytes accessed | tf_op | source)
XLA Modules:
  0.0 34.1 jit_solution(2547471049184918425)
XLA Ops:
  0.0 33.4 %shard_map.73 = bf16[256,128]{1,0:T(8,128)(2,1)S(1)} custom-call(bf16[256,2048]{1,0:T(8,128)(2,1)} %tok_hbm.1, bf16[3,2048,512]{2,1,0:T(8,128)(2,1)} %bitcast.2, bf16[512,2048]{1,0:T(8,128)(2,1)} %wout_hbm.1, f32[1,2048]{1,0:T(1,128)} %bitcast.3, bf16[2048,128]{1,0:T(8,128)(2,1)} %wlabel_hbm.1, s32[4]{0:T(128)} %off_mid.1, s32[4]{0:T(128)} %off_far.1), custom_call_target="tpu_custom_call" | custom-call | tf_op jit(solution)/shard_map/pallas_call | solution.py:416
  33.4 0.7 %convert_element_type.3 = f32[256,128]{1,0:T(8,128)} convert(bf16[256,128]{1,0:T(8,128)(2,1)S(1)} %shard_map.73) | non-fusion elementwise | flops 32768 | bytes 196608 | tf_op jit(solution)/shard_map/convert_element_type | solution.py:452

commit v4 on v3

--- a/solution.py
+++ b/solution.py
@@ -119,9 +119,17 @@
     return summed / total, top + jnp.log(total)
 
 
+def repeat(first, last, step):
+    def run(i, carry):
+        step(i)
+        return carry
+
+    lax.fori_loop(first, last, run, 0)
+
+
 def kernel(
     tok_hbm, wqkv_hbm, wout_hbm, gain_hbm, wlabel_hbm, off_mid, off_far, out_ref,
-    tok, wqkv, wout, gain, wlabel, qkv, pair_out, pair_in, ret_o, ret_l, got_o, got_l,
+    tok, wqkv, wout, gain, wlabel, qkv, near_o, near_l, pair_out, pair_in, ret_o, ret_l, got_o, got_l,
     attn, parts, sib_in, x_out, x_in, log_out, log_in,
     load_sem, w_sem, a2a_send, a2a_recv, o_send, o_recv, l_send, l_recv,
     sib_send, sib_recv, x_send, x_recv, log_send, log_recv,
@@ -150,23 +158,24 @@
         )
 
     wide = wqkv.shape[2]
-    halves = qkv.shape[2] // wide
-    loads = [pltpu.make_async_copy(tok_hbm, tok, load_sem.at[0])]
-    w_loads = []
+    halves = wqkv.shape[0] // 3
+    ready = heads // halves
+    loads = [
+        pltpu.make_async_copy(tok_hbm, tok, load_sem.at[0]),
+        pltpu.make_async_copy(wout_hbm, wout, load_sem.at[1]),
+        pltpu.make_async_copy(gain_hbm, gain, load_sem.at[2]),
+        pltpu.make_async_copy(wlabel_hbm, wlabel, load_sem.at[3]),
+    ]
+
+    def w_load(half, c):
+        cols = pl.ds(pl.multiple_of(half * wide, wide), wide)
+        k = half * 3 + c
+        return pltpu.make_async_copy(wqkv_hbm.at[c, :, cols], wqkv.at[k], w_sem.at[k])
+
+    loads[0].start()
     for half in range(halves):
         for c in range(3):
-            k = half * 3 + c
-            w_loads.append(
-                pltpu.make_async_copy(
-                    wqkv_hbm.at[c, :, pl.ds(half * wide, wide)], wqkv.at[k], w_sem.at[k]
-                )
-            )
-    loads.append(pltpu.make_async_copy(wout_hbm, wout, load_sem.at[1]))
-    loads.append(pltpu.make_async_copy(gain_hbm, gain, load_sem.at[2]))
-    loads.append(pltpu.make_async_copy(wlabel_hbm, wlabel, load_sem.at[3]))
-    loads[0].start()
-    for load in w_loads:
-        load.start()
+            w_load(half, c).start()
 
     def pair_copy(j):
         return pltpu.make_async_remote_copy(
@@ -187,55 +196,60 @@
     sel_row = jnp.where(is_mid, both, both - picked) * SPAN
     sel_tok = lax.broadcasted_iota(jnp.int32, (2 * picked, rows), 1)
     loads[0].wait()
-    for half in range(halves):
-        for c in range(3):
-            k = half * 3 + c
-            w_loads[k].wait()
-            qkv[c, :, half * wide : (half + 1) * wide] = jnp.dot(
-                tok[...], wqkv[k], preferred_element_type=jnp.float32
+
+    def project_half(half):
+        def project(c):
+            w_load(half, c).wait()
+            result = jnp.dot(
+                tok[...], wqkv[half * 3 + c], preferred_element_type=jnp.float32
             ).astype(jnp.bfloat16)
-        if half == halves - 1:
-            for load in loads[1:]:
-                load.start()
-        if half == 0:
+            for i in range(ready):
+                qkv[c, half * ready + i] = result[:, i * hd : (i + 1) * hd]
+
+        repeat(0, 3, project)
+
+        @pl.when(half == 0)
+        def _():
             pl.semaphore_wait(barrier, n_seq + n_head - 2)
-        for h in range(half * wide // hd, (half + 1) * wide // hd):
-            cols = slice(h * hd, (h + 1) * hd)
-            mine = jnp.concatenate([qkv[c, :, cols] for c in range(3)], axis=1)
+
+        for i in range(ready):
+            h = half * ready + i
+            mine = jnp.concatenate([qkv[c, h] for c in range(3)], axis=1)
             spot = sel_row + jnp.where(is_mid, off_mid[h], off_far[h])
             one_hot = (sel_tok == spot).astype(jnp.bfloat16)
             found = jnp.dot(one_hot, mine, preferred_element_type=jnp.float32).astype(
                 jnp.bfloat16
             )
             for b in range(2):
-                j = b * heads + h
-                pair_out[j] = found[b * picked : (b + 1) * picked]
-        ready = heads // halves
-        for d in range(2 * ready):
+                pair_out[b * heads + h] = found[b * picked : (b + 1) * picked]
+
+        def send(d):
             turn = lax.rem(seq + d, 2 * ready)
             j = turn // ready * heads + half * ready + lax.rem(turn, ready)
 
             @pl.when(seq != j)
-            def _(j=j):
+            def _():
                 pair_copy(j).start()
 
+        repeat(0, 2 * ready, send)
+
+    repeat(0, halves, project_half)
+    for load in loads[1:]:
+        load.start()
     pair_in[seq] = pair_out[seq]
 
     chunks = x_in.shape[0]
     part = x_in.shape[1]
     width = x_in.shape[2]
     side = 2 * part
-    firsts = ((1 - chip) * side, chip * side)
-
-    def near_rows(s, h):
-        place = pl.ds(pl.multiple_of(firsts[s], side), side)
-        cols = slice(h * hd, (h + 1) * hd)
-        return softmax_parts(qkv[0, place, cols], qkv[1, :, cols], qkv[2, :, cols])
-
-    near = [[near_rows(0, h) for h in range(heads // 2)], []]
-
-    for d in range(1, n_seq):
-        pair_arrival(lax.rem(seq + d, n_seq)).wait_recv()
+    def near_head(h):
+        o, lse = softmax_parts(qkv[0, h], qkv[1, h], qkv[2, h])
+        near_o[h] = o
+        near_l[h] = lse
+
+    repeat(0, heads, near_head)
+
+    repeat(1, n_seq, lambda d: pair_arrival(lax.rem(seq + d, n_seq)).wait_recv())
 
     everyone = n_seq * picked
     pq, pk, pv = (
@@ -259,55 +273,49 @@
             device_id=(i, head), device_id_type=MESH,
         )
 
-    outward = sorted(range(1, n_seq), key=lambda d: abs(2 * d - n_seq))
-    for d in outward:
-        o_copy(lax.rem(seq + d, n_seq), seq).start()
+    repeat(1, n_seq, lambda d: o_copy(lax.rem(seq + d, n_seq), seq).start())
 
     r0 = lax.broadcasted_iota(jnp.int32, (everyone, everyone), 0)
     r1 = lax.broadcasted_iota(jnp.int32, (everyone, everyone), 1)
     lse_row = jnp.sum(jnp.where(r0 == r1, lse, 0.0), axis=0, keepdims=True)
     for t in range(everyone // hd):
         ret_l[t] = lse_row[:, t * hd : (t + 1) * hd]
-    for d in outward:
-        l_copy(lax.rem(seq + d, n_seq), seq).start()
+    repeat(1, n_seq, lambda d: l_copy(lax.rem(seq + d, n_seq), seq).start())
 
     got_o[seq] = ret_o[seq]
     got_l[seq] = ret_l[seq // per_tile]
-    near[0] += [near_rows(0, h) for h in range(heads // 2, heads)]
 
     base = lax.rem(seq, per_tile) * picked
 
-    def merge(s, first):
+    def merge(s, first, h):
         tok_col = lax.broadcasted_iota(jnp.int32, (side, hd), 0) + first
         lane = lax.broadcasted_iota(jnp.int32, (side, hd), 1) - base
         tok_sel = lax.broadcasted_iota(jnp.int32, (side, picked), 0) + first
         row_sel = lax.broadcasted_iota(jnp.int32, (side, picked), 1)
         tok_one = lax.broadcasted_iota(jnp.int32, (side, 1), 0)
-        merged = []
-        for h in range(heads):
-            terms = [near[s][h]]
-            marks = [None]
-            for b, off in enumerate((off_mid, off_far)):
-                j = b * heads + h
-                spot = off[h]
-                hit = lane * SPAN + spot == tok_col
-                lse_col = jnp.sum(jnp.where(hit, got_l[j], 0.0), axis=-1, keepdims=True)
-                one_hot = (tok_sel == row_sel * SPAN + spot).astype(jnp.bfloat16)
-                spread = jnp.dot(one_hot, got_o[j], preferred_element_type=jnp.float32)
-                mark = lax.rem(tok_one, SPAN) == spot
-                terms.append((spread, jnp.where(mark, lse_col, -1e30)))
-                marks.append(mark)
-            peak = jnp.maximum(jnp.maximum(terms[0][1], terms[1][1]), terms[2][1])
-            upper = jnp.zeros((side, hd), jnp.float32)
-            lower = jnp.zeros((side, 1), jnp.float32)
-            for (o, lse), mark in zip(terms, marks):
-                factor = jnp.exp(lse - peak)
-                if mark is not None:
-                    factor = jnp.where(mark, factor, 0.0)
-                upper = upper + factor * o
-                lower = lower + factor
-            merged.append((upper / lower).astype(jnp.bfloat16))
-        return jnp.concatenate(merged, axis=1)
+        place = pl.ds(pl.multiple_of(first, side), side)
+        terms = [(near_o[h, place, :], near_l[h, place, :])]
+        marks = [None]
+        for b, off in enumerate((off_mid, off_far)):
+            j = b * heads + h
+            spot = off[h]
+            hit = lane * SPAN + spot == tok_col
+            lse_col = jnp.sum(jnp.where(hit, got_l[j], 0.0), axis=-1, keepdims=True)
+            one_hot = (tok_sel == row_sel * SPAN + spot).astype(jnp.bfloat16)
+            spread = jnp.dot(one_hot, got_o[j], preferred_element_type=jnp.float32)
+            mark = lax.rem(tok_one, SPAN) == spot
+            terms.append((spread, jnp.where(mark, lse_col, -1e30)))
+            marks.append(mark)
+        peak = jnp.maximum(jnp.maximum(terms[0][1], terms[1][1]), terms[2][1])
+        upper = jnp.zeros((side, hd), jnp.float32)
+        lower = jnp.zeros((side, 1), jnp.float32)
+        for (o, lse), mark in zip(terms, marks):
+            factor = jnp.exp(lse - peak)
+            if mark is not None:
+                factor = jnp.where(mark, factor, 0.0)
+            upper = upper + factor * o
+            lower = lower + factor
+        return (upper / lower).astype(jnp.bfloat16)
 
     def sib_copy(s, n):
         return pltpu.make_async_remote_copy(
@@ -332,34 +340,49 @@
 
     for load in loads[1:]:
         load.wait()
-    for d in range(1, n_seq):
+    def returned(d):
         j = lax.rem(seq + d, n_seq)
         o_copy(j, j).wait_recv()
         l_copy(j, j).wait_recv()
-    for s in range(2):
-        if s == 1:
-            near[1] = [near_rows(1, h) for h in range(heads)]
-        attn[s] = merge(s, firsts[s])
-        for n in range(chunks):
+
+    repeat(1, n_seq, returned)
+
+    def project_side(s):
+        first = lax.rem(1 - chip + s, 2) * side
+
+        def merge_pair(g):
+            for i in range(2):
+                h = 2 * g + i
+                attn[s, :, pl.ds(pl.multiple_of(h * hd, hd), hd)] = merge(s, first, h)
+
+        repeat(0, heads // 2, merge_pair)
+
+        def project_out(n):
+            cols = pl.ds(pl.multiple_of(n * width, width), width)
             parts[s, n] = (
-                jnp.dot(
-                    attn[s], wout[:, n * width : (n + 1) * width],
-                    preferred_element_type=jnp.float32,
-                )
+                jnp.dot(attn[s], wout[:, cols], preferred_element_type=jnp.float32)
                 .astype(jnp.bfloat16)
                 .reshape(2, part, width)
             )
             sib_copy(s, n).start()
-            if s == 0 and n > 0:
+
+            @pl.when((s == 0) & (n > 0))
+            def _():
                 pass_on(n - 1)
-        if s == 0:
+
+        repeat(0, chunks, project_out)
+
+        @pl.when(s == 0)
+        def _():
             pass_on(chunks - 1)
 
-    squares = jnp.zeros((part, 1), jnp.float32)
-    product = jnp.zeros((part, wlabel.shape[1]), jnp.float32)
+    repeat(0, 2, project_side)
+
     here = pl.ds(pl.multiple_of(head * part, part), part)
-    for n in range(chunks):
-        cols = slice(n * width, (n + 1) * width)
+
+    def finish(n, carry):
+        squares, product = carry
+        cols = pl.ds(pl.multiple_of(n * width, width), width)
         sib_copy(1, n).wait_recv()
         x_copy(n).wait_recv()
         summed = parts[1, n, core].astype(jnp.float32) + sib_in[1, n].astype(jnp.float32)
@@ -367,6 +390,14 @@
         squares = squares + jnp.sum(mixed * mixed, axis=-1, keepdims=True)
         scaled = (mixed * gain[:, cols]).astype(jnp.bfloat16)
         product = product + jnp.dot(scaled, wlabel[cols, :], preferred_element_type=jnp.float32)
+        return squares, product
+
+    squares, product = lax.fori_loop(
+        0,
+        chunks,
+        finish,
+        (jnp.zeros((part, 1), jnp.float32), jnp.zeros((part, wlabel.shape[1]), jnp.float32)),
+    )
     log_out[...] = (product / jnp.sqrt(squares / tok.shape[1] + 1e-05)).astype(jnp.bfloat16)
 
     def log_copy(p, slot):
@@ -385,16 +416,20 @@
     for p in range(n_head):
         out_ref[p * part : (p + 1) * part, :] = log_in[p]
 
-    for d in range(1, n_seq):
+    def sent(d):
         j = lax.rem(seq + d, n_seq)
         pair_copy(j).wait_send()
         o_copy(j, seq).wait_send()
         l_copy(j, seq).wait_send()
 
-    for n in range(chunks):
+    repeat(1, n_seq, sent)
+
+    def sent_parts(n):
         sib_copy(0, n).wait_send()
         sib_copy(1, n).wait_send()
         x_copy(n).wait_send()
+
+    repeat(0, chunks, sent_parts)
     for d in range(1, n_head):
         log_copy(lax.rem(head + d, n_head), head).wait_send()
 
@@ -424,7 +459,9 @@
             pltpu.VMEM((own, width), bf16),
             pltpu.VMEM((1, width), f32),
             pltpu.VMEM((width, classes), bf16),
-            pltpu.VMEM((3, rows, own), bf16),
+            pltpu.VMEM((3, heads, rows, hd), bf16),
+            pltpu.VMEM((heads, rows, hd), f32),
+            pltpu.VMEM((heads, rows, 1), f32),
             pltpu.VMEM((n_seq, picked, 3 * hd), bf16),
             pltpu.VMEM((n_seq, picked, 3 * hd), bf16),
             pltpu.VMEM((n_seq, picked, hd), bf16),

time: 34.2 us -> 33.4 us (0.977)
  Pallas kernels: 33.4 us -> 32.6 us
    pallas_call x1, Pallas kernels: 33.4 us -> 32.6 us  [fused_body(): pl.pallas_call(kernel, out_shape=pltpu.VMEM((rows, classes), bf16), in_sp...]
where the time goes in v4:
time: 33.4 us; the launch traced here: 33.2 us
  Pallas kernels  32.6 us (98%)
  other arithmetic  0.67 us (2%)
    pallas_call x1, Pallas kernels, fused_body(): pl.pallas_call(kernel, out_shape=pltpu.VMEM((rows, classes), bf16), in_sp...  32.6 us

profile of v4, /device:TPU:0, one launch (start us, length us, event | category | flops | bytes accessed | tf_op | source)
XLA Modules:
  0.0 33.2 jit_solution(9081465494801728628)
XLA Ops:
  0.0 32.6 %shard_map.73 = bf16[256,128]{1,0:T(8,128)(2,1)S(1)} custom-call(bf16[256,2048]{1,0:T(8,128)(2,1)} %tok_hbm.1, bf16[3,2048,512]{2,1,0:T(8,128)(2,1)} %bitcast.2, bf16[512,2048]{1,0:T(8,128)(2,1)} %wout_hbm.1, f32[1,2048]{1,0:T(1,128)} %bitcast.3, bf16[2048,128]{1,0:T(8,128)(2,1)} %wlabel_hbm.1, s32[4]{0:T(128)} %off_mid.1, s32[4]{0:T(128)} %off_far.1), custom_call_target="tpu_custom_call" | custom-call | tf_op jit(solution)/shard_map/pallas_call | solution.py:451
  32.6 0.7 %convert_element_type.3 = f32[256,128]{1,0:T(8,128)} convert(bf16[256,128]{1,0:T(8,128)(2,1)S(1)} %shard_map.73) | non-fusion elementwise | flops 32768 | bytes 196608 | tf_op jit(solution)/shard_map/convert_element_type | solution.py:489

commit v5 on v4

--- a/solution.py
+++ b/solution.py
@@ -140,7 +140,7 @@
     n_head = log_in.shape[0]
     rows = tok.shape[0]
     picked = pair_in.shape[1]
-    hd = got_o.shape[2]
+    hd = got_o.shape[3]
     heads = n_seq // 2
     core = lax.rem(head, 2)
     chip = head // 2
@@ -251,47 +251,53 @@
 
     repeat(1, n_seq, lambda d: pair_arrival(lax.rem(seq + d, n_seq)).wait_recv())
 
-    everyone = n_seq * picked
-    pq, pk, pv = (
-        pair_in[:, :, c * hd : (c + 1) * hd].reshape(everyone, hd) for c in range(3)
-    )
-    o, lse = softmax_parts(pq, pk, pv)
-    ret_o[...] = o.astype(jnp.bfloat16).reshape(n_seq, picked, hd)
-    per_tile = hd // picked
-
-    def o_copy(i, slot):
-        return pltpu.make_async_remote_copy(
-            src_ref=ret_o.at[i], dst_ref=got_o.at[slot],
-            send_sem=o_send.at[i], recv_sem=o_recv.at[slot],
+    half_picked = picked // 2
+    asked = n_seq * half_picked
+
+    def o_copy(s, i, slot):
+        return pltpu.make_async_remote_copy(
+            src_ref=ret_o.at[s, i], dst_ref=got_o.at[s, slot],
+            send_sem=o_send.at[s, i], recv_sem=o_recv.at[s, slot],
             device_id=(i, head), device_id_type=MESH,
         )
 
-    def l_copy(i, slot):
-        return pltpu.make_async_remote_copy(
-            src_ref=ret_l.at[i // per_tile], dst_ref=got_l.at[slot],
-            send_sem=l_send.at[i], recv_sem=l_recv.at[slot],
+    def l_copy(s, i, slot):
+        return pltpu.make_async_remote_copy(
+            src_ref=ret_l.at[s], dst_ref=got_l.at[s, slot],
+            send_sem=l_send.at[s, i], recv_sem=l_recv.at[s, slot],
             device_id=(i, head), device_id_type=MESH,
         )
 
-    repeat(1, n_seq, lambda d: o_copy(lax.rem(seq + d, n_seq), seq).start())
-
-    r0 = lax.broadcasted_iota(jnp.int32, (everyone, everyone), 0)
-    r1 = lax.broadcasted_iota(jnp.int32, (everyone, everyone), 1)
-    lse_row = jnp.sum(jnp.where(r0 == r1, lse, 0.0), axis=0, keepdims=True)
-    for t in range(everyone // hd):
-        ret_l[t] = lse_row[:, t * hd : (t + 1) * hd]
-    repeat(1, n_seq, lambda d: l_copy(lax.rem(seq + d, n_seq), seq).start())
-
-    got_o[seq] = ret_o[seq]
-    got_l[seq] = ret_l[seq // per_tile]
-
-    base = lax.rem(seq, per_tile) * picked
+    def answer(s):
+        first = lax.rem(1 - chip + s, 2) * half_picked
+        place = pl.ds(pl.multiple_of(first, half_picked), half_picked)
+        pq = pair_in[:, place, 0:hd].reshape(asked, hd)
+        pk, pv = (
+            pair_in[:, :, c * hd : (c + 1) * hd].reshape(n_seq * picked, hd) for c in (1, 2)
+        )
+        o, lse = softmax_parts(pq, pk, pv)
+        ret_o[s] = o.astype(jnp.bfloat16).reshape(n_seq, half_picked, hd)
+        r0 = lax.broadcasted_iota(jnp.int32, (asked, asked), 0)
+        r1 = lax.broadcasted_iota(jnp.int32, (asked, asked), 1)
+        ret_l[s] = jnp.sum(jnp.where(r0 == r1, lse, 0.0), axis=0, keepdims=True)
+
+        def send_back(d):
+            i = lax.rem(seq + d, n_seq)
+            o_copy(s, i, seq).start()
+            l_copy(s, i, seq).start()
+
+        repeat(1, n_seq, send_back)
+        got_o[s, seq] = ret_o[s, seq]
+        got_l[s, seq] = ret_l[s]
+
+    repeat(0, 2, answer)
+    base = seq * half_picked
 
     def merge(s, first, h):
-        tok_col = lax.broadcasted_iota(jnp.int32, (side, hd), 0) + first
+        tok_col = lax.broadcasted_iota(jnp.int32, (side, hd), 0)
         lane = lax.broadcasted_iota(jnp.int32, (side, hd), 1) - base
-        tok_sel = lax.broadcasted_iota(jnp.int32, (side, picked), 0) + first
-        row_sel = lax.broadcasted_iota(jnp.int32, (side, picked), 1)
+        tok_sel = lax.broadcasted_iota(jnp.int32, (side, half_picked), 0)
+        row_sel = lax.broadcasted_iota(jnp.int32, (side, half_picked), 1)
         tok_one = lax.broadcasted_iota(jnp.int32, (side, 1), 0)
         place = pl.ds(pl.multiple_of(first, side), side)
         terms = [(near_o[h, place, :], near_l[h, place, :])]
@@ -300,9 +306,9 @@
             j = b * heads + h
             spot = off[h]
             hit = lane * SPAN + spot == tok_col
-            lse_col = jnp.sum(jnp.where(hit, got_l[j], 0.0), axis=-1, keepdims=True)
+            lse_col = jnp.sum(jnp.where(hit, got_l[s, j], 0.0), axis=-1, keepdims=True)
             one_hot = (tok_sel == row_sel * SPAN + spot).astype(jnp.bfloat16)
-            spread = jnp.dot(one_hot, got_o[j], preferred_element_type=jnp.float32)
+            spread = jnp.dot(one_hot, got_o[s, j], preferred_element_type=jnp.float32)
             mark = lax.rem(tok_one, SPAN) == spot
             terms.append((spread, jnp.where(mark, lse_col, -1e30)))
             marks.append(mark)
@@ -340,15 +346,15 @@
 
     for load in loads[1:]:
         load.wait()
-    def returned(d):
-        j = lax.rem(seq + d, n_seq)
-        o_copy(j, j).wait_recv()
-        l_copy(j, j).wait_recv()
-
-    repeat(1, n_seq, returned)
-
     def project_side(s):
         first = lax.rem(1 - chip + s, 2) * side
+
+        def returned(d):
+            j = lax.rem(seq + d, n_seq)
+            o_copy(s, j, j).wait_recv()
+            l_copy(s, j, j).wait_recv()
+
+        repeat(1, n_seq, returned)
 
         def merge_pair(g):
             for i in range(2):
@@ -419,8 +425,9 @@
     def sent(d):
         j = lax.rem(seq + d, n_seq)
         pair_copy(j).wait_send()
-        o_copy(j, seq).wait_send()
-        l_copy(j, seq).wait_send()
+        for s in range(2):
+            o_copy(s, j, seq).wait_send()
+            l_copy(s, j, seq).wait_send()
 
     repeat(1, n_seq, sent)
 
@@ -464,10 +471,10 @@
             pltpu.VMEM((heads, rows, 1), f32),
             pltpu.VMEM((n_seq, picked, 3 * hd), bf16),
             pltpu.VMEM((n_seq, picked, 3 * hd), bf16),
-            pltpu.VMEM((n_seq, picked, hd), bf16),
-            pltpu.VMEM((n_seq * picked // hd, 1, hd), f32),
-            pltpu.VMEM((n_seq, picked, hd), bf16),
-            pltpu.VMEM((n_seq, 1, hd), f32),
+            pltpu.VMEM((2, n_seq, picked // 2, hd), bf16),
+            pltpu.VMEM((2, 1, n_seq * picked // 2), f32),
+            pltpu.VMEM((2, n_seq, picked // 2, hd), bf16),
+            pltpu.VMEM((2, n_seq, 1, n_seq * picked // 2), f32),
             pltpu.VMEM((2, 2 * part, own), bf16),
             pltpu.VMEM((2, chunks, 2, part, span), bf16),
             pltpu.VMEM((2, chunks, part, span), bf16),
@@ -476,7 +483,7 @@
             pltpu.VMEM((part, classes), bf16),
             pltpu.VMEM((n_head, part, classes), bf16),
             dma((4,)), dma((6,)), dma((n_seq,)), dma((n_seq,)),
-            dma((n_seq,)), dma((n_seq,)), dma((n_seq,)), dma((n_seq,)),
+            dma((2, n_seq)), dma((2, n_seq)), dma((2, n_seq)), dma((2, n_seq)),
             dma((2, chunks)), dma((2, chunks)), dma((chunks,)), dma((chunks,)),
             dma((n_head,)), dma((n_head,)),
         ],

time: 33.4 us -> 33.2 us (level)
  no operation moved by 1% of the time
where the time goes in v5:
time: 33.2 us; the launch traced here: 33 us
  Pallas kernels  32.4 us (98%)
  other arithmetic  0.67 us (2%)
    pallas_call x1, Pallas kernels, fused_body(): pl.pallas_call(kernel, out_shape=pltpu.VMEM((rows, classes), bf16), in_sp...  32.4 us
    convert_element_type x1, other arithmetic, fused_body(): return pl.pallas_call(kernel, out_shape=pltpu.VMEM((rows, classes), bf16)...  0.67 us

profile of v5, /device:TPU:0, one launch (start us, length us, event | category | flops | bytes accessed | tf_op | source)
XLA Modules:
  0.0 33.0 jit_solution(910301738393161670)
XLA Ops:
  0.0 32.4 %shard_map.73 = bf16[256,128]{1,0:T(8,128)(2,1)S(1)} custom-call(bf16[256,2048]{1,0:T(8,128)(2,1)} %tok_hbm.1, bf16[3,2048,512]{2,1,0:T(8,128)(2,1)} %bitcast.2, bf16[512,2048]{1,0:T(8,128)(2,1)} %wout_hbm.1, f32[1,2048]{1,0:T(1,128)} %bitcast.3, bf16[2048,128]{1,0:T(8,128)(2,1)} %wlabel_hbm.1, s32[4]{0:T(128)} %off_mid.1, s32[4]{0:T(128)} %off_far.1), custom_call_target="tpu_custom_call" | custom-call | tf_op jit(solution)/shard_map/pallas_call | solution.py:458
  32.4 0.7 %convert_element_type.3 = f32[256,128]{1,0:T(8,128)} convert(bf16[256,128]{1,0:T(8,128)(2,1)S(1)} %shard_map.73) | non-fusion elementwise | flops 32768 | bytes 196608 | tf_op jit(solution)/shard_map/convert_element_type | solution.py:496

commit v6 on v5

--- a/solution.py
+++ b/solution.py
@@ -247,7 +247,7 @@
         near_o[h] = o
         near_l[h] = lse
 
-    repeat(0, heads, near_head)
+    repeat(0, heads // 2, near_head)
 
     repeat(1, n_seq, lambda d: pair_arrival(lax.rem(seq + d, n_seq)).wait_recv())
 
@@ -291,6 +291,7 @@
         got_l[s, seq] = ret_l[s]
 
     repeat(0, 2, answer)
+    repeat(heads // 2, heads, near_head)
     base = seq * half_picked
 
     def merge(s, first, h):

time: 33.2 us -> 33.2 us (level)
  no operation moved by 1% of the time
where the time goes in v6:
time: 33.2 us; the launch traced here: 33 us
  Pallas kernels  32.4 us (98%)
  other arithmetic  0.67 us (2%)
    pallas_call x1, Pallas kernels, fused_body(): pl.pallas_call(kernel, out_shape=pltpu.VMEM((rows, classes), bf16), in_sp...  32.4 us
    convert_element_type x1, other arithmetic, fused_body(): return pl.pallas_call(kernel, out_shape=pltpu.VMEM((rows, classes), bf16)...  0.67 us

profile of v6, /device:TPU:0, one launch (start us, length us, event | category | flops | bytes accessed | tf_op | source)
XLA Modules:
  0.0 33.0 jit_solution(9464855863165458802)
XLA Ops:
  0.0 32.4 %shard_map.73 = bf16[256,128]{1,0:T(8,128)(2,1)S(1)} custom-call(bf16[256,2048]{1,0:T(8,128)(2,1)} %tok_hbm.1, bf16[3,2048,512]{2,1,0:T(8,128)(2,1)} %bitcast.2, bf16[512,2048]{1,0:T(8,128)(2,1)} %wout_hbm.1, f32[1,2048]{1,0:T(1,128)} %bitcast.3, bf16[2048,128]{1,0:T(8,128)(2,1)} %wlabel_hbm.1, s32[4]{0:T(128)} %off_mid.1, s32[4]{0:T(128)} %off_far.1), custom_call_target="tpu_custom_call" | custom-call | tf_op jit(solution)/shard_map/pallas_call | solution.py:459
  32.4 0.7 %convert_element_type.3 = f32[256,128]{1,0:T(8,128)} convert(bf16[256,128]{1,0:T(8,128)(2,1)S(1)} %shard_map.73) | non-fusion elementwise | flops 32768 | bytes 196608 | tf_op jit(solution)/shard_map/convert_element_type | solution.py:497
